TPU v7x, 256 devices: a whole 4x4x8 slice. The times are simulated.
256 devices in a mesh: tm: 32 (over y, x, core), tile: 8 (over z).
Axes of the slice: x: 4, y: 4, z: 8, core: 2. Of those that a mesh axis runs over, the one named last changes fastest.
Arguments:
- input_frames: bfloat16 [256, 128, 256, 128], P('tm', 'tile'), may hold values from -24 to 24
- clip_spans: int32 [16], replicated, may hold values from 1 to 8, 64 in all
- conv_weight: bfloat16 [3, 3, 3, 128, 128], replicated, may hold values from -0.109375 to 0.109375
- norm_gain: float32 [128], replicated, may hold values from 0.5 to 1.5
- norm_bias: float32 [128], replicated, may hold values from -0.5 to 0.5
Outputs:
- output_frames: bfloat16 [128, 64, 128, 128], P('tm', 'tile')
All inputs are finite; a program needn't handle non-finite values.
Results may differ from a plain program's by a relative error of at most 0.001.
Values may be sent and summed in bfloat16 or wider, within the bound.
A program may use at most 128 MiB of HBM per device.

v0:
```python
import jax
import jax.numpy as jnp
from jax import lax
from jax.sharding import PartitionSpec as P

G = 32
F = 4
CH_DEV = 2


def passed_along(x, axis, by):
    size = lax.axis_size(axis)
    pairs = [(i, i + by) for i in range(size) if 0 <= i + by < size]
    return lax.ppermute(x, axis, pairs)


def apply_taps(extended, conv_weight, time_taps, out_start, out_count, offset):
    frame_axis = extended.ndim - 4
    first_tap = time_taps[0]
    tap_count = len(time_taps)
    first_frame = 2 * out_start + first_tap - offset
    selected = lax.slice_in_dim(
        extended, first_frame, first_frame + 2 * (out_count - 1) + tap_count, 1, frame_axis
    )
    leading = selected.shape[:frame_axis]
    result = lax.conv_general_dilated(
        selected,
        conv_weight,
        (2, 2, 2),
        [(0, 0), (0, 0), (0, 0)],
        dimension_numbers=("NDHWC", "DHWIO", "NDHWC"),
        preferred_element_type=jnp.float32,
    )
    return result.reshape(leading + result.shape[1:])


def with_margin(block, rim_rows):
    stacked = jnp.concatenate([rim_rows[..., None, :, :], block], axis=-3)
    left_pad = jnp.zeros(stacked.shape[:-2] + (1, stacked.shape[-1]), stacked.dtype)
    return jnp.concatenate([left_pad, stacked], axis=-2)


def body(input_frames, clip_spans, conv_weight, norm_gain, norm_bias):
    frames, height_in, width_in, channels = input_frames.shape
    clip_count = clip_spans.shape[0]
    blocks = input_frames.reshape(CH_DEV, F, height_in, width_in, channels)
    slot_ids = lax.axis_index("tm") * CH_DEV + jnp.arange(CH_DEV, dtype=jnp.int32)
    clip_ends = jnp.cumsum(clip_spans)
    starts = clip_ends - clip_spans
    slot_clip = jnp.sum((slot_ids[:, None] >= clip_ends[None, :]).astype(jnp.int32), axis=1)
    is_start = jnp.any(slot_ids[:, None] == starts[None, :], axis=1)
    tail_block = passed_along(blocks[CH_DEV - 1, F - 2 :], "tm", 1)
    pieces = []
    for member in range(CH_DEV):
        first_pair = jnp.stack([blocks[member, 0], blocks[member, 0]])
        prior = tail_block if member == 0 else blocks[member - 1, F - 2 :]
        prior_pair = jnp.where(is_start[member], first_pair, prior)
        pieces.append(jnp.concatenate([prior_pair, blocks[member]], axis=0))
    extended = jnp.stack(pieces)
    rim_rows = passed_along(extended[:, :, height_in - 1], "tile", 1)
    extended = with_margin(extended, rim_rows)
    conv_out = apply_taps(extended, conv_weight, (0, 1, 2), 0, F // 2, 0)
    high = lax.Precision.HIGHEST
    group_size = channels // G
    slot_to_clip = (slot_clip[:, None] == jnp.arange(clip_count, dtype=jnp.int32)[None, :]).astype(
        jnp.float32
    )
    grouping = (
        jnp.arange(channels, dtype=jnp.int32)[:, None] // group_size
        == jnp.arange(G, dtype=jnp.int32)[None, :]
    ).astype(jnp.float32)
    counts = clip_spans.astype(jnp.float32) * (
        F // 2 * (height_in // 2) * lax.axis_size("tile") * (width_in // 2) * group_size
    )

    def to_groups(per_slot):
        return jnp.dot(jnp.dot(slot_to_clip.T, per_slot, precision=high), grouping, precision=high)

    def to_channels(per_clip):
        return jnp.dot(jnp.dot(slot_to_clip, per_clip, precision=high), grouping.T, precision=high)

    channel_sums = jnp.sum(conv_out, axis=(1, 2, 3))
    totals = lax.psum(to_groups(channel_sums), ("tm", "tile"))
    means = totals / counts[:, None]
    centered = conv_out - to_channels(means)[:, None, None, None, :]
    spread = lax.psum(to_groups(jnp.sum(centered * centered, axis=(1, 2, 3))), ("tm", "tile"))
    variance = spread / counts[:, None]
    inverse = to_channels(lax.rsqrt(variance + 1e-06))
    normed = centered * inverse[:, None, None, None, :] * norm_gain + norm_bias
    output = jax.nn.silu(normed).astype(jnp.bfloat16)
    return output.reshape(CH_DEV * (F // 2), height_in // 2, width_in // 2, channels)


def solution(mesh):
    in_specs = (P("tm", "tile", None, None), P(), P(), P(), P())
    out_specs = P("tm", "tile", None, None)
    return jax.shard_map(body, mesh=mesh, in_specs=in_specs, out_specs=out_specs, check_vma=False)
```

profile of v0, /device:TPU:1, one launch (start us, length us, event | category | flops | bytes accessed | tf_op | source)
XLA Modules:
  0.0 315.1 jit_solution(12342127719952090810)
XLA Ops:
  0.0 3.3 %slice_bitcast_fusion.1 = bf16[2,16,256,128]{3,2,1,0:T(8,128)(2,1)} fusion(bf16[2,4,16,256,128]{4,3,2,1,0:T(8,128)(2,1)} %bitcast.48), kind=kLoop, calls=%fused_computation.17 | loop fusion | bytes 4194304 | tf_op jit(solution)/shard_map/squeeze | solution.py:52
  3.3 4.5 %collective-permute-start = (bf16[2,16,256,128]{3,2,1,0:T(8,128)(2,1)}, bf16[2,16,256,128]{3,2,1,0:T(8,128)(2,1)}, u32[]{:S(2)}, u32[]{:S(2)}) collective-permute-start(bf16[2,16,256,128]{3,2,1,0:T(8,128)(2,1)} %slice_bitcast_fusion.1), channel_id=1, source_target_pairs={{0,8},{8,16},{16,24},{24,32},{32,40},{40,48},{48,56},{56,64},{64,7... | collective-permute-start | bytes 6291464 | tf_op jit(solution)/shard_map/ppermute | solution.py:14
  8.2 0.7 fusion.38
  8.9 1.8 slice_bitcast_fusion.4
  10.7 3.0 fusion.6
  13.8 2.3 fusion.37
  16.7 14.4 %collective-permute-done = bf16[2,16,256,128]{3,2,1,0:T(8,128)(2,1)} collective-permute-done((bf16[2,16,256,128]{3,2,1,0:T(8,128)(2,1)}, bf16[2,16,256,128]{3,2,1,0:T(8,128)(2,1)}, u32[]{:S(2)}, u32[]{:S(2)}) %collective-permute-start) | collective-permute-done | bytes 2097184 | tf_op jit(solution)/shard_map/ppermute | solution.py:14
  31.0 2.3 maximum_select_fusion
  33.3 3.4 %maximum_bitcast_fusion.1 = bf16[1,6,16,256,128]{4,3,2,1,0:T(8,128)(2,1)S(1)} fusion(bf16[4,16,256,128]{3,2,1,0:T(8,128)(2,1)} %get-tuple-element.7, bf16[2,16,256,128]{3,2,1,0:T(8,128)(2,1)} %maximum_select_fusion), kind=kLoop, calls=%fused_computation.6 | loop fusion | flops 3145728 | bytes 12582912 | tf_op jit(solution)/shard_map/stack | solution.py:59
  36.8 3.8 %collective-permute-start.1 = (bf16[2,6,256,128]{3,2,1,0:T(8,128)(2,1)S(1)}, bf16[2,6,256,128]{3,2,1,0:T(8,128)(2,1)S(1)}, u32[]{:S(2)}, u32[]{:S(2)}) collective-permute-start(bf16[2,6,256,128]{3,2,1,0:T(8,128)(2,1)S(1)} %fusion.11), channel_id=1, source_target_pairs={{0,1},{1,2},{2,3},{3,4},{4,5},{5,6},{6,7},{8,9},{9,10},{10,11},{11... | collective-permute-start | bytes 2359304 | tf_op jit(solution)/shard_map/ppermute | solution.py:14
  40.8 8.5 %collective-permute-done.1 = bf16[2,6,256,128]{3,2,1,0:T(8,128)(2,1)S(1)} collective-permute-done((bf16[2,6,256,128]{3,2,1,0:T(8,128)(2,1)S(1)}, bf16[2,6,256,128]{3,2,1,0:T(8,128)(2,1)S(1)}, u32[]{:S(2)}, u32[]{:S(2)}) %collective-permute-start.1) | collective-permute-done | bytes 786464 | tf_op jit(solution)/shard_map/ppermute | solution.py:14
  49.3 1.7 maximum_bitcast_fusion
  51.0 29.9 %copy.40 = bf16[6,17,2,256,128]{4,2,3,1,0:T(2,128)(2,1)} copy(bf16[6,17,2,256,128]{4,3,1,0,2:T(8,128)(2,1)S(1)} %maximum_bitcast_fusion) | data formatting | bytes 26738688
  81.0 16.1 %pad.1.clone = bf16[6,17,2,272,128]{4,2,3,1,0:T(2,128)(2,1)S(1)} pad(bf16[6,17,2,256,128]{4,2,3,1,0:T(2,128)(2,1)} %copy.40, bf16[]{:T(256)} %constant.42), padding=0_0x0_0x0_0x1_15x0_0 | pad | bytes 27574274 | tf_op jit(solution)/shard_map/concatenate | solution.py:38
  97.6 32.7 %fusion = bf16[6,17,2,8,36,128]{5,2,4,3,1,0:T(2,128)(2,1)} fusion(bf16[6,17,2,7,2,128]{5,2,4,3,1,0:T(2,128)(2,1)S(1)} %slice.49, bf16[6,17,2,8,34,128]{5,2,4,3,1,0:T(2,128)(2,1)S(1)} %bitcast.47), kind=kLoop, calls=%fused_computation.1 | loop fusion | flops 45121536 | bytes 29976576 | tf_op jit(solution)/shard_map/conv_general_dilated | solution.py:26
  130.4 12.0 %fusion.7 = f32[2,8,16,17,128]{4,2,3,1,0:T(8,128)S(1)} fusion(bf16[3,3,3,128,128]{4,3,2,1,0:T(8,128)(2,1)S(1)} %copy-done, bf16[6,17,2,8,36,128]{5,2,4,3,1,0:T(2,128)(2,1)} %fusion, pred[16,17]{0,1:T(8,128)(4,1)S(1)} %copy-done.7), kind=kOutput, calls=%fused_computation.19 | convolution fusion | flops 3850928128 | bytes 18153744 | tf_op jit(solution)/shard_map/conv_general_dilated | solution.py:26
  142.4 0.7 copy.33
  143.8 89.9 %psum.14 = f32[16,32]{1,0:T(8,128)S(1)} all-reduce(f32[16,32]{1,0:T(8,128)S(1)} %fusion.15), channel_id=1, replica_groups=mesh['tm'=32,'tile'=8] {'tm','tile'}, use_global_device_ids=true, to_apply=%region_4.5 | all-reduce | flops 512 | bytes 4096 | tf_op jit(solution)/shard_map/psum | solution.py:83
  234.9 0.9 copy-done.2
  235.8 0.7 copy.35
  237.2 73.7 %psum.15 = f32[16,32]{1,0:T(8,128)S(1)} all-reduce(f32[16,32]{1,0:T(8,128)S(1)} %fusion.13), channel_id=1, replica_groups=mesh['tm'=32,'tile'=8] {'tm','tile'}, use_global_device_ids=true, to_apply=%region_6.7 | all-reduce | flops 512 | bytes 4096 | tf_op jit(solution)/shard_map/psum | solution.py:86
  311.5 1.0 copy-done.3
  312.5 1.0 multiply_convert_fusion
  313.8 1.2 copy.38
  (41 shorter events, 5.4 us)
Async XLA Ops:
  0.0 130.4 %copy-start = (bf16[3,3,3,128,128]{4,3,2,1,0:T(8,128)(2,1)S(1)}, bf16[3,3,3,128,128]{4,3,2,1,0:T(8,128)(2,1)}, u32[]{:S(2)}) copy-start(bf16[3,3,3,128,128]{4,3,2,1,0:T(8,128)(2,1)} %param.7) | copy-start | bytes 2654212
  0.0 7.8 %copy-start.6 = (s32[16]{0:T(128)S(1)}, s32[16]{0:T(128)}, u32[]{:S(2)}) copy-start(s32[16]{0:T(128)} %param.6) | copy-start | bytes 196
  3.3 27.8 %collective-permute-start = (bf16[2,16,256,128]{3,2,1,0:T(8,128)(2,1)}, bf16[2,16,256,128]{3,2,1,0:T(8,128)(2,1)}, u32[]{:S(2)}, u32[]{:S(2)}) collective-permute-start(bf16[2,16,256,128]{3,2,1,0:T(8,128)(2,1)} %slice_bitcast_fusion.1), channel_id=1, source_target_pairs={{0,8},{8,16},{16,24},{24,32},{32,40},{40,48},{48,56},{56,64},{64,7... | collective-permute-start | bytes 6291464 | tf_op jit(solution)/shard_map/ppermute | solution.py:14
  8.9 4.9 %copy-start.1 = (bf16[8,16,256,128]{3,2,1,0:T(8,128)(2,1)S(1)}, bf16[8,16,256,128]{3,2,1,0:T(8,128)(2,1)}, u32[]{:S(2)}) copy-start(bf16[8,16,256,128]{3,2,1,0:T(8,128)(2,1)} %param.5) | copy-start | bytes 25165828
  36.8 12.5 %collective-permute-start.1 = (bf16[2,6,256,128]{3,2,1,0:T(8,128)(2,1)S(1)}, bf16[2,6,256,128]{3,2,1,0:T(8,128)(2,1)S(1)}, u32[]{:S(2)}, u32[]{:S(2)}) collective-permute-start(bf16[2,6,256,128]{3,2,1,0:T(8,128)(2,1)S(1)} %fusion.11), channel_id=1, source_target_pairs={{0,1},{1,2},{2,3},{3,4},{4,5},{5,6},{6,7},{8,9},{9,10},{10,11},{11... | collective-permute-start | bytes 2359304 | tf_op jit(solution)/shard_map/ppermute | solution.py:14
  97.6 32.8 %copy-start.7 = (pred[16,17]{0,1:T(8,128)(4,1)S(1)}, pred[16,17]{0,1:T(8,128)(4,1)}, u32[]{:S(2)}) copy-start(pred[16,17]{0,1:T(8,128)(4,1)} %constant.46) | copy-start | bytes 820
  234.4 1.4 copy-start.2
  236.4 75.1 %copy-start.4 = (f32[128]{0:T(128)S(1)}, f32[128]{0:T(128)}, u32[]{:S(2)}) copy-start(f32[128]{0:T(128)} %param.9) | copy-start | bytes 1540
  236.4 75.1 %copy-start.5 = (f32[128]{0:T(128)S(1)}, f32[128]{0:T(128)}, u32[]{:S(2)}) copy-start(f32[128]{0:T(128)} %param.8) | copy-start | bytes 1540
  310.9 1.6 copy-start.3
where the time goes:
time: 316 us; the launch traced here: 315 us
  blocking collectives  164 us (52%)
  local copies, waits for them, and re-layouts  60 us (19%)
  other arithmetic  46.4 us (15%)
  waiting for transfers between devices  22.9 us (7%)
  matrix products  13.7 us (4%)
  starting transfers between devices  8.27 us (3%)
    psum x1, blocking collectives, body(): totals = lax.psum(to_groups(channel_sums), ('tm', 'tile'))  89.9 us
    psum x1, blocking collectives, body(): lax.psum(to_groups(jnp.sum(centered * centered, axis=(1, 2, 3))), ('tm',...  73.7 us
    conv_general_dilated x1, other arithmetic, apply_taps(): lax.conv_general_dilated(selected, conv_weight, (2, 2, 2), [(0, 0), (0, 0...  32.7 us
    unnamed x17, local copies, waits for them, and re-layouts  31.8 us
    ppermute x2, waiting for transfers between devices, passed_along(): return lax.ppermute(x, axis, pairs)  22.9 us
    concatenate x1, local copies, waits for them, and re-layouts, with_margin(): stacked = jnp.concatenate([rim_rows[..., None, :, :], block], axis=-3)  16.1 us
    conv_general_dilated x1, matrix products, apply_taps(): lax.conv_general_dilated(selected, conv_weight, (2, 2, 2), [(0, 0), (0, 0...  12 us
    ppermute x2, starting transfers between devices, passed_along(): return lax.ppermute(x, axis, pairs)  8.27 us
  transfers between devices with their start and end apart: 2, of which 2 were waited for; matrix products, arithmetic and copies ran while one was open for 3% of the time, Pallas kernels for 0%

commit v1 on v0

v1 whole, which is shorter than its diff:
```python
import functools

import jax
import jax.numpy as jnp
from jax import lax
from jax.experimental import pallas as pl
from jax.experimental.pallas import tpu as pltpu
from jax.sharding import PartitionSpec as P

F = 4
CH_DEV = 2
GROUP = 4
REACH = 4
EPS = 1e-6
MESH = pl.DeviceIdType.MESH
f32, bf16 = jnp.float32, jnp.bfloat16


def kernel(
    n_tm, n_tile, rows, cols, chans,
    spans, x_hbm, w_hbm, y_hbm, stat_out,
    xb, xe, xo, wt, y, p_send, c_send, p_recv, c_recv, z_send, z_recv,
    mine, from_tile, pooled, from_tm,
    in_sem, w_sem, out_sem, ps_sem, pr_sem, cs_sem, cr_sem, zs_sem, zr_sem,
    as_sem, ar_sem, bs_sem, br_sem,
):
    tm, tile = lax.axis_index("tm"), lax.axis_index("tile")
    half, c2 = rows // 2, 2 * chans
    m_rows = half * cols
    reach = [k for k in range(-REACH, REACH + 1) if k]

    def at_tm(k):
        return {"tm": lax.rem(tm + k + n_tm, n_tm)}

    def at_tile(k):
        return {"tile": lax.rem(tile + k, n_tile)}

    def remote(src, dst, send, recv, where):
        return pltpu.make_async_remote_copy(
            src_ref=src, dst_ref=dst, send_sem=send, recv_sem=recv, device_id=where, device_id_type=MESH
        )

    order = (6, 7, 0, 4, 5, 2, 3, 1)
    loads = {f: pltpu.make_async_copy(x_hbm.at[f], xb.at[f], in_sem.at[f]) for f in order}
    w_loads = [
        pltpu.make_async_copy(w_hbm.at[:, 1], wt.at[:, 0:chans, 0:chans], w_sem.at[0]),
        pltpu.make_async_copy(w_hbm.at[:, 2], wt.at[:, chans:c2, 0:chans], w_sem.at[1]),
        pltpu.make_async_copy(w_hbm.at[:, 0], wt.at[:, chans:c2, chans:c2], w_sem.at[2]),
    ]
    loads[6].start()
    for copy in w_loads:
        copy.start()
    for f in order[1:]:
        loads[f].start()

    barrier = pltpu.get_barrier_semaphore()
    for k in range(1, n_tile):
        pl.semaphore_signal(barrier, inc=1, device_id=at_tile(k), device_id_type=MESH)
    for k in reach:
        pl.semaphore_signal(barrier, inc=1, device_id=at_tm(k), device_id_type=MESH)

    ends, total = [], jnp.int32(0)
    for c in range(spans.shape[0]):
        total = total + spans[c]
        ends.append(total)
    lows, highs = [], []
    for m in range(CH_DEV):
        slot = tm * CH_DEV + m
        lo, hi = jnp.int32(0), jnp.int32(n_tm * CH_DEV)
        for end in ends:
            lo = jnp.maximum(lo, jnp.where(end <= slot, end, 0))
            hi = jnp.minimum(hi, jnp.where(end > slot, end, n_tm * CH_DEV))
        lows.append(lo)
        highs.append(hi)
    opens = [(lows[m] == tm * CH_DEV + m) for m in range(CH_DEV)]

    wt[:, 0:chans, chans:c2] = jnp.zeros((wt.shape[0], chans, chans), bf16)
    for f in range(xo.shape[0]):
        xo[f, 0] = jnp.zeros((cols, c2), bf16)

    def pair_columns(raw, f):
        for r in range(rows):
            pair = raw(r).reshape(cols, c2)
            if r % 2:
                xo[f, 1 + r // 2] = pair
            else:
                xe[f, r // 2] = pair

    def joined(both):
        moved = pltpu.roll(both[:, chans:c2], 1, 0)
        column = lax.broadcasted_iota(jnp.int32, moved.shape, 0) % cols
        return both[:, 0:chans] + jnp.where(column == 0, 0.0, moved)

    def taps(pairs, first=0, count=None):
        count = half if count is None else count
        sums = None
        for a, f in pairs:
            for b, part in ((0, xo[f, first : first + count]), (1, xe[f, first : first + count]),
                            (2, xo[f, first + 1 : first + 1 + count])):
                one = jnp.dot(part.reshape(count * cols, c2), wt[3 * a + b], preferred_element_type=f32)
                sums = one if sums is None else sums + one
        return joined(sums)

    def below(pairs):
        sums = None
        for a, f in pairs:
            one = jnp.dot(xo[f, half], wt[3 * a], preferred_element_type=f32)
            sums = one if sums is None else sums + one
        return joined(sums)

    def ready(f):
        loads[f].wait()
        pair_columns(lambda r: xb[f, r], f)

    ready(6)
    ready(7)
    for copy in w_loads:
        copy.wait()

    passed = ((0, 6), (1, 7))
    c_send[...] = below(passed)
    quarter = half // 2
    p_send[0] = taps(passed, 0, quarter)
    pl.semaphore_wait(barrier, n_tile - 1 + len(reach))
    corner = remote(c_send, c_recv, cs_sem, cr_sem, at_tm(1))
    corner.start()
    partial = [remote(p_send.at[i], p_recv.at[i], ps_sem.at[i], pr_sem.at[i], at_tm(1)) for i in range(2)]
    partial[0].start()
    p_send[1] = taps(passed, quarter, quarter)
    partial[1].start()

    edge = [remote(z_send.at[k], z_recv.at[k], zs_sem.at[k], zr_sem.at[k], at_tile(1)) for k in range(4)]

    ready(0)
    y[0] = taps(((2, 0),))
    own = taps(((0, 0), (1, 0)))
    p_own = own
    z_first = below(((2, 0),))
    z_own = below(((0, 0), (1, 0)))

    ready(4)
    ready(5)
    z_send[3] = below(((0, 4), (1, 5), (2, 6)))
    edge[3].start()
    y[3] = taps(((0, 4), (1, 5), (2, 6)))

    corner.wait_recv()
    z_send[0] = z_first + jnp.where(opens[0], z_own, c_recv[...])
    edge[0].start()

    ready(2)
    loads[3].wait()
    pair_columns(lambda r: jnp.where(opens[1], xb[4, r], xb[3, r]), 3)
    pair_columns(lambda r: jnp.where(opens[1], xb[4, r], xb[2, r]), 8)
    z_send[2] = below(((0, 8), (1, 3), (2, 4)))
    edge[2].start()
    y[2] = taps(((0, 8), (1, 3), (2, 4)))

    ready(1)
    z_send[1] = below(((0, 0), (1, 1), (2, 2)))
    edge[1].start()
    y[1] = taps(((0, 0), (1, 1), (2, 2)))

    stores = [pltpu.make_async_copy(y.at[k], y_hbm.at[k], out_sem.at[k]) for k in range(4)]

    def finish(k):
        edge[k].wait_recv()
        y[k, 0:cols] = y[k, 0:cols] + jnp.where(tile == 0, 0.0, z_recv[k])
        if k == 0:
            for i in range(2):
                partial[i].wait_recv()
                part = pl.ds(i * quarter * cols, quarter * cols)
                y[k, part] = y[k, part] + jnp.where(opens[0], p_own[i * quarter * cols : (i + 1) * quarter * cols], p_recv[i])
        stores[k].start()
        mean = jnp.sum(y[k], axis=0, keepdims=True) * (1.0 / m_rows)
        off = y[k] - mean
        return mean, jnp.sum(off * off, axis=0, keepdims=True)

    def pool(means, squares, count):
        mean = functools.reduce(jnp.add, means) * (1.0 / len(means))
        apart = functools.reduce(jnp.add, [(m - mean) * (m - mean) for m in means])
        return mean, functools.reduce(jnp.add, squares) + count * apart

    part = [None] * 4
    for k in (3, 2, 1, 0):
        part[k] = finish(k)
    count = m_rows
    blocks = [pool([part[2 * m][0], part[2 * m + 1][0]], [part[2 * m][1], part[2 * m + 1][1]], count) for m in range(CH_DEV)]
    count *= 2

    fill = jnp.zeros((8 - 2 * CH_DEV, chans), f32)

    def packed(stats):
        return jnp.concatenate([s[0] for s in stats] + [s[1] for s in stats] + [fill], axis=0)

    mine[...] = packed(blocks)
    to_tiles = [
        remote(mine, from_tile.at[k - 1], as_sem.at[k - 1], ar_sem.at[k - 1], at_tile(k)) for k in range(1, n_tile)
    ]
    for copy in to_tiles:
        copy.start()
    for copy in to_tiles:
        copy.wait_recv()
    all_means = [mine[0:CH_DEV]] + [from_tile[k, 0:CH_DEV] for k in range(n_tile - 1)]
    all_squares = [mine[CH_DEV : 2 * CH_DEV]] + [from_tile[k, CH_DEV : 2 * CH_DEV] for k in range(n_tile - 1)]
    mean, square = pool(all_means, all_squares, count)
    count *= n_tile
    pooled[...] = jnp.concatenate([mean, square, fill], axis=0)

    to_tm = [remote(pooled, from_tm.at[i], bs_sem.at[i], br_sem.at[i], at_tm(k)) for i, k in enumerate(reach)]
    for copy in to_tm:
        copy.start()
    for copy in to_tm:
        copy.wait_recv()
    held = [(tm, pooled[...])] + [(tm - k, from_tm[i]) for i, k in enumerate(reach)]

    lane = lax.broadcasted_iota(jnp.int32, (1, chans), 1)

    def over_group(v):
        step = 1
        while step < GROUP:
            v = v + jnp.where((lane // step) % 2 == 1, pltpu.roll(v, step, 1), pltpu.roll(v, chans - step, 1))
            step *= 2
        return v

    rows_out = []
    for m in range(CH_DEV):
        shares = []
        for device, stats in held:
            for q in range(CH_DEV):
                slot = device * CH_DEV + q
                inside = jnp.logical_and(slot >= lows[m], slot < highs[m])
                shares.append((inside, stats[q : q + 1], stats[CH_DEV + q : CH_DEV + q + 1]))
        spans_here = jnp.full((1, chans), (highs[m] - lows[m]).astype(f32))
        clip_mean = functools.reduce(jnp.add, [jnp.where(i, a, 0.0) for i, a, _ in shares]) / spans_here
        mean = over_group(clip_mean) * (1.0 / GROUP)
        spread = functools.reduce(
            jnp.add, [jnp.where(i, s + count * ((a - mean) * (a - mean)), 0.0) for i, a, s in shares]
        )
        variance = over_group(spread) / (spans_here * float(count * GROUP))
        rows_out += [mean, lax.rsqrt(variance + EPS)]
    stat_out[...] = jnp.concatenate(rows_out + [fill], axis=0)

    for copy in stores:
        copy.wait()
    corner.wait_send()
    for copy in partial + edge + to_tiles + to_tm:
        copy.wait_send()


def body(input_frames, clip_spans, conv_weight, norm_gain, norm_bias):
    frames, rows, width, chans = input_frames.shape
    n_tm, n_tile = lax.axis_size("tm"), lax.axis_size("tile")
    half, cols = rows // 2, width // 2
    m_rows = half * cols
    weights = conv_weight.reshape(9, 3, chans, chans)
    n_reach = 2 * REACH
    dma = pltpu.SemaphoreType.DMA
    hbm, vmem = pl.BlockSpec(memory_space=pl.ANY), pl.BlockSpec(memory_space=pltpu.VMEM)
    y, stats = pl.pallas_call(
        functools.partial(kernel, n_tm, n_tile, rows, cols, chans),
        out_shape=[jax.ShapeDtypeStruct((4, m_rows, chans), f32), jax.ShapeDtypeStruct((8, chans), f32)],
        in_specs=[pl.BlockSpec(memory_space=pltpu.SMEM), hbm, hbm],
        out_specs=[hbm, vmem],
        scratch_shapes=[
            pltpu.VMEM((frames, rows, width, chans), bf16),
            pltpu.VMEM((frames + 1, half, cols, 2 * chans), bf16),
            pltpu.VMEM((frames + 1, half + 1, cols, 2 * chans), bf16),
            pltpu.VMEM((9, 2 * chans, 2 * chans), bf16),
            pltpu.VMEM((4, m_rows, chans), f32),
            pltpu.VMEM((2, m_rows // 2, chans), f32),
            pltpu.VMEM((cols, chans), f32),
            pltpu.VMEM((2, m_rows // 2, chans), f32),
            pltpu.VMEM((cols, chans), f32),
            pltpu.VMEM((4, cols, chans), f32),
            pltpu.VMEM((4, cols, chans), f32),
            pltpu.VMEM((8, chans), f32),
            pltpu.VMEM((n_tile - 1, 8, chans), f32),
            pltpu.VMEM((8, chans), f32),
            pltpu.VMEM((n_reach, 8, chans), f32),
            dma((frames,)), dma((3,)), dma((4,)),
            dma((2,)), dma((2,)), dma, dma, dma((4,)), dma((4,)),
            dma((n_tile - 1,)), dma((n_tile - 1,)), dma((n_reach,)), dma((n_reach,)),
        ],
        compiler_params=pltpu.CompilerParams(
            collective_id=0, has_side_effects=True, vmem_limit_bytes=56 * 2**20
        ),
    )(clip_spans, input_frames, weights)
    y = y.reshape(CH_DEV, F // 2, half, cols, chans)
    mean, inverse = stats[0:4:2].reshape(2, 1, 1, 1, chans), stats[1:4:2].reshape(2, 1, 1, 1, chans)
    normed = (y - mean) * inverse * norm_gain + norm_bias
    return jax.nn.silu(normed).astype(bf16).reshape(CH_DEV * (F // 2), half, cols, chans)


def solution(mesh):
    in_specs = (P("tm", "tile", None, None), P(), P(), P(), P())
    out_specs = P("tm", "tile", None, None)
    return jax.shard_map(body, mesh=mesh, in_specs=in_specs, out_specs=out_specs, check_vma=False)
```

time: 316 us -> 41.7 us (0.13)
  blocking collectives: 164 us -> 0 us
  local copies, waits for them, and re-layouts: 60 us -> 1.39 us
  other arithmetic: 46.4 us -> 3.25 us
  Pallas kernels: 0 us -> 36.9 us
  waiting for transfers between devices: 22.9 us -> 0 us
  matrix products: 13.7 us -> 0 us
  starting transfers between devices: 8.27 us -> 0 us
    psum x2 -> x0, blocking collectives: 164 us -> none  [the longest x1 89.9 us: body(): totals = lax.psum(to_groups(channel_sums), ('tm', 'tile'))]
    pallas_call x0 -> x1, Pallas kernels: none -> 36.9 us  [body(): pl.pallas_call(functools.partial(kernel, n_tm, n_tile, rows, cols, chans)...]
    conv_general_dilated x1 -> x0, other arithmetic: 32.7 us -> none  [apply_taps(): lax.conv_general_dilated(selected, conv_weight, (2, 2, 2), [(0, 0), (0, 0...]
    unnamed x17 -> x4, local copies, waits for them, and re-layouts: 31.8 us -> 0.01 us
    ppermute x2 -> x0, waiting for transfers between devices: 22.9 us -> none  [passed_along(): return lax.ppermute(x, axis, pairs)]
    concatenate x1 -> x0, local copies, waits for them, and re-layouts: 16.1 us -> none  [with_margin(): stacked = jnp.concatenate([rim_rows[..., None, :, :], block], axis=-3)]
    conv_general_dilated x1 -> x0, matrix products: 12 us -> none  [apply_taps(): lax.conv_general_dilated(selected, conv_weight, (2, 2, 2), [(0, 0), (0, 0...]
    ppermute x2 -> x0, starting transfers between devices: 8.27 us -> none  [passed_along(): return lax.ppermute(x, axis, pairs)]
  transfers between devices with their start and end apart: 2 -> 0, of which waited for: 2 -> 0; matrix products, arithmetic and copies ran while one was open for 3% -> 0% of each run, Pallas kernels for 0% -> 0%
where the time goes in v1:
time: 41.7 us; the launch traced here: 41.5 us
  Pallas kernels  36.9 us (88%)
  other arithmetic  3.25 us (8%)
  local copies, waits for them, and re-layouts  1.39 us (3%)
    pallas_call x1, Pallas kernels, body(): pl.pallas_call(functools.partial(kernel, n_tm, n_tile, rows, cols, chans)...  36.9 us
    convert_element_type x1, other arithmetic, body(): jax.nn.silu(normed).astype(bf16)  3.25 us

profile of v1, /device:TPU:1, one launch (start us, length us, event | category | flops | bytes accessed | tf_op | source)
XLA Modules:
  0.0 41.5 jit_solution(4177540547201865445)
XLA Ops:
  0.0 0.0 copy-start
  0.0 0.0 copy-start.1
  0.0 36.9 %shard_map.55 = (f32[4,1024,128]{2,1,0:T(8,128)}, f32[8,128]{1,0:T(8,128)}) custom-call(s32[16]{0:T(128)} %spans.1, bf16[8,16,256,128]{3,2,1,0:T(8,128)(2,1)} %x_hbm.1, bf16[9,3,128,128]{3,2,1,0:T(8,128)(2,1)} %bitcast.5), custom_call_target="tpu_custom_call" | custom-call | tf_op jit(solution)/shard_map/pallas_call | solution.py:260
  36.9 0.7 %slice.7 = f32[2,128]{1,0:T(2,128)S(1)} slice(f32[8,128]{1,0:T(8,128)} %get-tuple-element.8), slice={[1:4:2], [0:128:1]} | slice | bytes 2048 | tf_op jit(solution)/shard_map/slice | solution.py:290
  37.6 0.7 %slice.6 = f32[2,128]{1,0:T(2,128)S(1)} slice(f32[8,128]{1,0:T(8,128)} %get-tuple-element.8), slice={[0:4:2], [0:128:1]} | slice | bytes 2048 | tf_op jit(solution)/shard_map/slice | solution.py:290
  38.3 0.0 copy-done
  38.3 0.0 copy-done.1
  38.3 3.3 %multiply_convert_fusion = bf16[4,8,128,128]{3,2,1,0:T(8,128)(2,1)} fusion(f32[4,8,128,128]{3,2,1,0:T(8,128)} %bitcast.4, f32[128]{0:T(128)S(1)} %copy-done, f32[128]{0:T(128)S(1)} %copy-done.1, f32[4,128]{1,0:T(4,128)S(1)} %bitcast.7, f32[4,128]{1,0:T(4,128)S(1)} %bitcast.6), kind=kLoop, calls=%fused_computation | loop fusion | flops 4718592 | bytes 3150848 | tf_op jit(solution)/shard_map/convert_element_type | solution.py:292
  (2 shorter events, 0.0 us)
Async XLA Ops:
  0.0 38.3 %copy-start = (f32[128]{0:T(128)S(1)}, f32[128]{0:T(128)}, u32[]{:S(2)}) copy-start(f32[128]{0:T(128)} %param.9) | copy-start | bytes 1540
  0.0 38.3 %copy-start.1 = (f32[128]{0:T(128)S(1)}, f32[128]{0:T(128)}, u32[]{:S(2)}) copy-start(f32[128]{0:T(128)} %param.8) | copy-start | bytes 1540

commit v2 on v1

--- a/solution.py
+++ b/solution.py
@@ -18,10 +18,10 @@
 
 def kernel(
     n_tm, n_tile, rows, cols, chans,
-    spans, x_hbm, w_hbm, y_hbm, stat_out,
-    xb, xe, xo, wt, y, p_send, c_send, p_recv, c_recv, z_send, z_recv,
+    spans_hbm, x_hbm, w_hbm, y, stat_out,
+    spans, xb, xe, xo, wt, p_own, p_send, c_send, p_recv, c_recv, z_send, z_recv,
     mine, from_tile, pooled, from_tm,
-    in_sem, w_sem, out_sem, ps_sem, pr_sem, cs_sem, cr_sem, zs_sem, zr_sem,
+    spans_sem, in_sem, w_sem, ps_sem, pr_sem, cs_sem, cr_sem, zs_sem, zr_sem,
     as_sem, ar_sem, bs_sem, br_sem,
 ):
     tm, tile = lax.axis_index("tm"), lax.axis_index("tile")
@@ -47,6 +47,8 @@
         pltpu.make_async_copy(w_hbm.at[:, 2], wt.at[:, chans:c2, 0:chans], w_sem.at[1]),
         pltpu.make_async_copy(w_hbm.at[:, 0], wt.at[:, chans:c2, chans:c2], w_sem.at[2]),
     ]
+    spans_load = pltpu.make_async_copy(spans_hbm, spans, spans_sem)
+    spans_load.start()
     loads[6].start()
     for copy in w_loads:
         copy.start()
@@ -59,6 +61,7 @@
     for k in reach:
         pl.semaphore_signal(barrier, inc=1, device_id=at_tm(k), device_id_type=MESH)
 
+    spans_load.wait()
     ends, total = [], jnp.int32(0)
     for c in range(spans.shape[0]):
         total = total + spans[c]
@@ -91,15 +94,17 @@
         column = lax.broadcasted_iota(jnp.int32, moved.shape, 0) % cols
         return both[:, 0:chans] + jnp.where(column == 0, 0.0, moved)
 
-    def taps(pairs, first=0, count=None):
-        count = half if count is None else count
-        sums = None
-        for a, f in pairs:
-            for b, part in ((0, xo[f, first : first + count]), (1, xe[f, first : first + count]),
-                            (2, xo[f, first + 1 : first + 1 + count])):
-                one = jnp.dot(part.reshape(count * cols, c2), wt[3 * a + b], preferred_element_type=f32)
-                sums = one if sums is None else sums + one
-        return joined(sums)
+    def taps(pairs, into):
+        step = half // 2
+        for part in range(2):
+            first = part * step
+            sums = None
+            for a, f in pairs:
+                for b, lhs in ((0, xo[f, first : first + step]), (1, xe[f, first : first + step]),
+                               (2, xo[f, first + 1 : first + 1 + step])):
+                    one = jnp.dot(lhs.reshape(step * cols, c2), wt[3 * a + b], preferred_element_type=f32)
+                    sums = one if sums is None else sums + one
+            into[first * cols : (first + step) * cols] = joined(sums)
 
     def below(pairs):
         sums = None
@@ -118,31 +123,31 @@
         copy.wait()
 
     passed = ((0, 6), (1, 7))
+    size = m_rows // 2
     c_send[...] = below(passed)
-    quarter = half // 2
-    p_send[0] = taps(passed, 0, quarter)
+    taps(passed, p_send)
     pl.semaphore_wait(barrier, n_tile - 1 + len(reach))
     corner = remote(c_send, c_recv, cs_sem, cr_sem, at_tm(1))
     corner.start()
-    partial = [remote(p_send.at[i], p_recv.at[i], ps_sem.at[i], pr_sem.at[i], at_tm(1)) for i in range(2)]
-    partial[0].start()
-    p_send[1] = taps(passed, quarter, quarter)
-    partial[1].start()
+    partial = [
+        remote(p_send.at[pl.ds(i * size, size)], p_recv.at[pl.ds(i * size, size)], ps_sem.at[i], pr_sem.at[i], at_tm(1))
+        for i in range(2)
+    ]
+    for copy in partial:
+        copy.start()
 
     edge = [remote(z_send.at[k], z_recv.at[k], zs_sem.at[k], zr_sem.at[k], at_tile(1)) for k in range(4)]
 
     ready(0)
-    y[0] = taps(((2, 0),))
-    own = taps(((0, 0), (1, 0)))
-    p_own = own
-    z_first = below(((2, 0),))
-    z_own = below(((0, 0), (1, 0)))
-
     ready(4)
     ready(5)
     z_send[3] = below(((0, 4), (1, 5), (2, 6)))
+    z_first = below(((2, 0),))
+    z_own = below(((0, 0), (1, 0)))
+    taps(((2, 0),), y.at[0])
+    taps(((0, 0), (1, 0)), p_own)
+    taps(((0, 4), (1, 5), (2, 6)), y.at[3])
     edge[3].start()
-    y[3] = taps(((0, 4), (1, 5), (2, 6)))
 
     corner.wait_recv()
     z_send[0] = z_first + jnp.where(opens[0], z_own, c_recv[...])
@@ -152,26 +157,21 @@
     loads[3].wait()
     pair_columns(lambda r: jnp.where(opens[1], xb[4, r], xb[3, r]), 3)
     pair_columns(lambda r: jnp.where(opens[1], xb[4, r], xb[2, r]), 8)
+    ready(1)
     z_send[2] = below(((0, 8), (1, 3), (2, 4)))
+    z_send[1] = below(((0, 0), (1, 1), (2, 2)))
     edge[2].start()
-    y[2] = taps(((0, 8), (1, 3), (2, 4)))
-
-    ready(1)
-    z_send[1] = below(((0, 0), (1, 1), (2, 2)))
     edge[1].start()
-    y[1] = taps(((0, 0), (1, 1), (2, 2)))
-
-    stores = [pltpu.make_async_copy(y.at[k], y_hbm.at[k], out_sem.at[k]) for k in range(4)]
+    taps(((0, 8), (1, 3), (2, 4)), y.at[2])
+    taps(((0, 0), (1, 1), (2, 2)), y.at[1])
 
     def finish(k):
         edge[k].wait_recv()
         y[k, 0:cols] = y[k, 0:cols] + jnp.where(tile == 0, 0.0, z_recv[k])
         if k == 0:
-            for i in range(2):
-                partial[i].wait_recv()
-                part = pl.ds(i * quarter * cols, quarter * cols)
-                y[k, part] = y[k, part] + jnp.where(opens[0], p_own[i * quarter * cols : (i + 1) * quarter * cols], p_recv[i])
-        stores[k].start()
+            for copy in partial:
+                copy.wait_recv()
+            y[k] = y[k] + jnp.where(opens[0], p_own[...], p_recv[...])
         mean = jnp.sum(y[k], axis=0, keepdims=True) * (1.0 / m_rows)
         off = y[k] - mean
         return mean, jnp.sum(off * off, axis=0, keepdims=True)
@@ -241,11 +241,22 @@
         rows_out += [mean, lax.rsqrt(variance + EPS)]
     stat_out[...] = jnp.concatenate(rows_out + [fill], axis=0)
 
-    for copy in stores:
-        copy.wait()
     corner.wait_send()
     for copy in partial + edge + to_tiles + to_tm:
         copy.wait_send()
+
+
+def finishing(y, stats, gain, bias, out_hbm, out, sem):
+    copies = []
+    for k in range(y.shape[0]):
+        m = k // (F // 2)
+        normed = (y[k] - stats[2 * m : 2 * m + 1]) * stats[2 * m + 1 : 2 * m + 2] * gain[...] + bias[...]
+        halved = 0.5 * normed
+        out[k] = (halved * jnp.tanh(halved) + halved).astype(bf16)
+        copies.append(pltpu.make_async_copy(out.at[k], out_hbm.at[k], sem.at[k]))
+        copies[-1].start()
+    for copy in copies:
+        copy.wait()
 
 
 def body(input_frames, clip_spans, conv_weight, norm_gain, norm_bias):
@@ -253,43 +264,59 @@
     n_tm, n_tile = lax.axis_size("tm"), lax.axis_size("tile")
     half, cols = rows // 2, width // 2
     m_rows = half * cols
+    outs = CH_DEV * (F // 2)
     weights = conv_weight.reshape(9, 3, chans, chans)
     n_reach = 2 * REACH
     dma = pltpu.SemaphoreType.DMA
-    hbm, vmem = pl.BlockSpec(memory_space=pl.ANY), pl.BlockSpec(memory_space=pltpu.VMEM)
+    any_space, vmem = pl.BlockSpec(memory_space=pl.ANY), pl.BlockSpec(memory_space=pltpu.VMEM)
     y, stats = pl.pallas_call(
         functools.partial(kernel, n_tm, n_tile, rows, cols, chans),
-        out_shape=[jax.ShapeDtypeStruct((4, m_rows, chans), f32), jax.ShapeDtypeStruct((8, chans), f32)],
-        in_specs=[pl.BlockSpec(memory_space=pltpu.SMEM), hbm, hbm],
-        out_specs=[hbm, vmem],
+        out_shape=[pltpu.VMEM((outs, m_rows, chans), f32), pltpu.VMEM((8, chans), f32)],
+        in_specs=[any_space] * 3,
+        out_specs=[vmem, vmem],
         scratch_shapes=[
+            pltpu.SMEM(clip_spans.shape, jnp.int32),
             pltpu.VMEM((frames, rows, width, chans), bf16),
             pltpu.VMEM((frames + 1, half, cols, 2 * chans), bf16),
             pltpu.VMEM((frames + 1, half + 1, cols, 2 * chans), bf16),
             pltpu.VMEM((9, 2 * chans, 2 * chans), bf16),
-            pltpu.VMEM((4, m_rows, chans), f32),
-            pltpu.VMEM((2, m_rows // 2, chans), f32),
+            pltpu.VMEM((m_rows, chans), f32),
+            pltpu.VMEM((m_rows, chans), f32),
             pltpu.VMEM((cols, chans), f32),
-            pltpu.VMEM((2, m_rows // 2, chans), f32),
+            pltpu.VMEM((m_rows, chans), f32),
             pltpu.VMEM((cols, chans), f32),
-            pltpu.VMEM((4, cols, chans), f32),
-            pltpu.VMEM((4, cols, chans), f32),
+            pltpu.VMEM((outs, cols, chans), f32),
+            pltpu.VMEM((outs, cols, chans), f32),
             pltpu.VMEM((8, chans), f32),
             pltpu.VMEM((n_tile - 1, 8, chans), f32),
             pltpu.VMEM((8, chans), f32),
             pltpu.VMEM((n_reach, 8, chans), f32),
-            dma((frames,)), dma((3,)), dma((4,)),
+            dma, dma((frames,)), dma((3,)),
             dma((2,)), dma((2,)), dma, dma, dma((4,)), dma((4,)),
             dma((n_tile - 1,)), dma((n_tile - 1,)), dma((n_reach,)), dma((n_reach,)),
         ],
         compiler_params=pltpu.CompilerParams(
-            collective_id=0, has_side_effects=True, vmem_limit_bytes=56 * 2**20
+            collective_id=0, has_side_effects=True, vmem_limit_bytes=48 * 2**20
         ),
-    )(clip_spans, input_frames, weights)
-    y = y.reshape(CH_DEV, F // 2, half, cols, chans)
-    mean, inverse = stats[0:4:2].reshape(2, 1, 1, 1, chans), stats[1:4:2].reshape(2, 1, 1, 1, chans)
-    normed = (y - mean) * inverse * norm_gain + norm_bias
-    return jax.nn.silu(normed).astype(bf16).reshape(CH_DEV * (F // 2), half, cols, chans)
+    )(
+        pltpu.with_memory_space_constraint(clip_spans, pltpu.HBM),
+        input_frames,
+        pltpu.with_memory_space_constraint(weights, pltpu.HBM),
+    )
+    out = pl.pallas_call(
+        finishing,
+        out_shape=jax.ShapeDtypeStruct((outs, m_rows, chans), bf16),
+        in_specs=[vmem] * 4,
+        out_specs=any_space,
+        scratch_shapes=[pltpu.VMEM((outs, m_rows, chans), bf16), dma((outs,))],
+        compiler_params=pltpu.CompilerParams(vmem_limit_bytes=16 * 2**20),
+    )(
+        pltpu.with_memory_space_constraint(y, pltpu.VMEM),
+        pltpu.with_memory_space_constraint(stats, pltpu.VMEM),
+        norm_gain.reshape(1, chans),
+        norm_bias.reshape(1, chans),
+    )
+    return out.reshape(outs, half, cols, chans)
 
 
 def solution(mesh):

time: 41.7 us -> 33.5 us (0.80)
  Pallas kernels: 36.9 us -> 33.4 us
  other arithmetic: 3.25 us -> 0 us
  local copies, waits for them, and re-layouts: 1.39 us -> 0.01 us
    pallas_call x1, Pallas kernels: 36.9 us -> 32 us  [body(): pl.pallas_call(functools.partial(kernel, n_tm, n_tile, rows, cols, chans)...]
    convert_element_type x1 -> x0, other arithmetic: 3.25 us -> none  [body(): jax.nn.silu(normed).astype(bf16)]
    slice x2 -> x0, local copies, waits for them, and re-layouts: 1.37 us -> none  [the longest x1 0.69 us: body(): stats[1:4:2].reshape(2, 1, 1, 1, chans)]
    pallas_call x0 -> x1, Pallas kernels: none -> 1.33 us  [body(): pl.pallas_call(finishing, out_shape=jax.ShapeDtypeStruct((outs, m_rows, c...]
where the time goes in v2:
time: 33.5 us; the launch traced here: 33.4 us
  Pallas kernels  33.4 us (100%)
    pallas_call x1, Pallas kernels, body(): pl.pallas_call(functools.partial(kernel, n_tm, n_tile, rows, cols, chans)...  32 us
    pallas_call x1, Pallas kernels, body(): pl.pallas_call(finishing, out_shape=jax.ShapeDtypeStruct((outs, m_rows, c...  1.33 us

profile of v2, /device:TPU:1, one launch (start us, length us, event | category | flops | bytes accessed | tf_op | source)
XLA Modules:
  0.0 33.4 jit_solution(13698564808155069155)
XLA Ops:
  0.0 0.0 copy-start.1
  0.0 0.0 copy-start
  0.0 32.0 %shard_map.55 = (f32[4,1024,128]{2,1,0:T(8,128)S(1)}, f32[8,128]{1,0:T(8,128)S(1)}) custom-call(s32[16]{0:T(128)} %spans_hbm.1, bf16[8,16,256,128]{3,2,1,0:T(8,128)(2,1)} %x_hbm.1, bf16[9,3,128,128]{3,2,1,0:T(8,128)(2,1)} %bitcast.6), custom_call_target="tpu_custom_call" | custom-call | tf_op jit(solution)/shard_map/pallas_call | solution.py:272
  32.1 0.0 copy-done.1
  32.1 0.0 copy-done
  32.1 1.3 %shard_map.56 = bf16[4,1024,128]{2,1,0:T(8,128)(2,1)} custom-call(f32[4,1024,128]{2,1,0:T(8,128)S(1)} %get-tuple-element.7.y, f32[8,128]{1,0:T(8,128)S(1)} %get-tuple-element.8.stats, f32[1,128]{1,0:T(1,128)S(1)} %bitcast.4, f32[1,128]{1,0:T(1,128)S(1)} %bitcast.5), custom_call_target="tpu_custom_call" | custom-call | tf_op jit(solution)/shard_map/pallas_call | solution.py:306
Async XLA Ops:
  0.0 32.1 %copy-start.1 = (f32[128]{0:T(128)S(1)}, f32[128]{0:T(128)}, u32[]{:S(2)}) copy-start(f32[128]{0:T(128)} %param.9) | copy-start | bytes 1540
  0.0 32.1 %copy-start = (f32[128]{0:T(128)S(1)}, f32[128]{0:T(128)}, u32[]{:S(2)}) copy-start(f32[128]{0:T(128)} %param.8) | copy-start | bytes 1540

commit v3 on v2

--- a/solution.py
+++ b/solution.py
@@ -12,6 +12,8 @@
 GROUP = 4
 REACH = 4
 EPS = 1e-6
+CODES = 32767.0
+TINY = 1e-30
 MESH = pl.DeviceIdType.MESH
 f32, bf16 = jnp.float32, jnp.bfloat16
 
@@ -19,21 +21,25 @@
 def kernel(
     n_tm, n_tile, rows, cols, chans,
     spans_hbm, x_hbm, w_hbm, y, stat_out,
-    spans, xb, xe, xo, wt, p_own, p_send, c_send, p_recv, c_recv, z_send, z_recv,
+    spans, rb, ro, xb, xe, xo, wt, p_own, p_raw, p_send, p_most, c_send, c_most, z_send, z_most,
+    p_recv, p_scale, c_recv, c_scale, z_recv, z_scale,
     mine, from_tile, pooled, from_tm,
-    spans_sem, in_sem, w_sem, ps_sem, pr_sem, cs_sem, cr_sem, zs_sem, zr_sem,
-    as_sem, ar_sem, bs_sem, br_sem,
+    spans_sem, row_sem, in_sem, w_sem, halo_send, halo_recv, as_sem, ar_sem, bs_sem, br_sem,
 ):
     tm, tile = lax.axis_index("tm"), lax.axis_index("tile")
     half, c2 = rows // 2, 2 * chans
     m_rows = half * cols
-    reach = [k for k in range(-REACH, REACH + 1) if k]
+    reach = [sign * k for k in range(REACH, 0, -1) for sign in (-1, 1)]
+    around = sorted(range(1, n_tile), key=lambda k: -min(k, n_tile - k))
 
     def at_tm(k):
         return {"tm": lax.rem(tm + k + n_tm, n_tm)}
 
     def at_tile(k):
         return {"tile": lax.rem(tile + k, n_tile)}
+
+    def aslant(k):
+        return {"tm": lax.rem(tm + k + n_tm, n_tm), "tile": lax.rem(tile + k + n_tile, n_tile)}
 
     def remote(src, dst, send, recv, where):
         return pltpu.make_async_remote_copy(
@@ -42,17 +48,22 @@
 
     order = (6, 7, 0, 4, 5, 2, 3, 1)
     loads = {f: pltpu.make_async_copy(x_hbm.at[f], xb.at[f], in_sem.at[f]) for f in order}
-    w_loads = [
-        pltpu.make_async_copy(w_hbm.at[:, 1], wt.at[:, 0:chans, 0:chans], w_sem.at[0]),
-        pltpu.make_async_copy(w_hbm.at[:, 2], wt.at[:, chans:c2, 0:chans], w_sem.at[1]),
-        pltpu.make_async_copy(w_hbm.at[:, 0], wt.at[:, chans:c2, chans:c2], w_sem.at[2]),
-    ]
+    w_loads = []
+    for a in range(3):
+        from_w, to_w = w_hbm.at[3 * a : 3 * a + 3], wt.at[3 * a : 3 * a + 3]
+        w_loads.append([
+            pltpu.make_async_copy(from_w.at[:, 1], to_w.at[:, 0:chans, 0:chans], w_sem.at[a, 0]),
+            pltpu.make_async_copy(from_w.at[:, 2], to_w.at[:, chans:c2, 0:chans], w_sem.at[a, 1]),
+            pltpu.make_async_copy(from_w.at[:, 0], to_w.at[:, chans:c2, chans:c2], w_sem.at[a, 2]),
+        ])
     spans_load = pltpu.make_async_copy(spans_hbm, spans, spans_sem)
+    row_load = pltpu.make_async_copy(x_hbm.at[:, rows - 1], rb, row_sem)
+    row_load.start()
+    for a in range(3):
+        for copy in w_loads[a]:
+            copy.start()
     spans_load.start()
-    loads[6].start()
-    for copy in w_loads:
-        copy.start()
-    for f in order[1:]:
+    for f in order:
         loads[f].start()
 
     barrier = pltpu.get_barrier_semaphore()
@@ -60,6 +71,8 @@
         pl.semaphore_signal(barrier, inc=1, device_id=at_tile(k), device_id_type=MESH)
     for k in reach:
         pl.semaphore_signal(barrier, inc=1, device_id=at_tm(k), device_id_type=MESH)
+    for k in (-1, 1):
+        pl.semaphore_signal(barrier, inc=1, device_id=aslant(k), device_id_type=MESH)
 
     spans_load.wait()
     ends, total = [], jnp.int32(0)
@@ -94,7 +107,7 @@
         column = lax.broadcasted_iota(jnp.int32, moved.shape, 0) % cols
         return both[:, 0:chans] + jnp.where(column == 0, 0.0, moved)
 
-    def taps(pairs, into):
+    def taps(pairs, into, add=False):
         step = half // 2
         for part in range(2):
             first = part * step
@@ -104,74 +117,95 @@
                                (2, xo[f, first + 1 : first + 1 + step])):
                     one = jnp.dot(lhs.reshape(step * cols, c2), wt[3 * a + b], preferred_element_type=f32)
                     sums = one if sums is None else sums + one
-            into[first * cols : (first + step) * cols] = joined(sums)
-
-    def below(pairs):
-        sums = None
-        for a, f in pairs:
-            one = jnp.dot(xo[f, half], wt[3 * a], preferred_element_type=f32)
-            sums = one if sums is None else sums + one
-        return joined(sums)
+            there = slice(first * cols, (first + step) * cols)
+            into[there] = into[there] + joined(sums) if add else joined(sums)
+
+    def encode(value, codes, there, most, r):
+        top = jnp.maximum(jnp.max(jnp.abs(value), axis=0, keepdims=True), TINY)
+        most[r : r + 1] = top
+        codes[there] = jnp.round(value * (CODES / top)).astype(jnp.int32).astype(jnp.int16)
+
+    def decode(codes, there, most, r):
+        return codes[there].astype(jnp.int32).astype(f32) * (most[r : r + 1] * (1.0 / CODES))
+
+    def row_of(r):
+        return slice(r * cols, (r + 1) * cols)
 
     def ready(f):
         loads[f].wait()
         pair_columns(lambda r: xb[f, r], f)
 
+    def w_ready(a):
+        for copy in w_loads[a]:
+            copy.wait()
+
+    row_load.wait()
+    for f in range(xb.shape[0]):
+        ro[f] = rb[f].reshape(cols, c2)
+    earlier = [jnp.where(opens[1], ro[4], ro[f]) for f in (2, 3)]
+    for a in range(3):
+        for copy in w_loads[a]:
+            copy.wait()
+    by_tap = [
+        jnp.dot(jnp.concatenate(stack, axis=0), wt[3 * a], preferred_element_type=f32)
+        for a, stack in enumerate((
+            [ro[0], earlier[0], ro[4], ro[0], ro[6]],
+            [ro[1], earlier[1], ro[5], ro[0], ro[7]],
+            [ro[2], ro[4], ro[6], ro[0]],
+        ))
+    ]
+    first_two = by_tap[0] + by_tap[1]
+    whole = joined(first_two[0 : 3 * cols] + by_tap[2][0 : 3 * cols])
+    own, aside = joined(first_two[3 * cols : 4 * cols]), joined(first_two[4 * cols : 5 * cols])
+    z_most[...] = jnp.zeros_like(z_most)
+    c_most[...] = jnp.zeros_like(c_most)
+    encode(joined(by_tap[2][3 * cols : 4 * cols]) + jnp.where(opens[0], own, 0.0), z_send, row_of(0), z_most, 0)
+    for k in (1, 2, 3):
+        encode(whole[row_of(k - 1)], z_send, row_of(k), z_most, k)
+    encode(aside, c_send, row_of(0), c_most, 0)
+
     ready(6)
     ready(7)
-    for copy in w_loads:
-        copy.wait()
-
-    passed = ((0, 6), (1, 7))
+    taps(((0, 6), (1, 7)), p_raw)
+    for r in range(half):
+        encode(p_raw[row_of(r)], p_send, row_of(r), p_most, r)
     size = m_rows // 2
-    c_send[...] = below(passed)
-    taps(passed, p_send)
-    pl.semaphore_wait(barrier, n_tile - 1 + len(reach))
-    corner = remote(c_send, c_recv, cs_sem, cr_sem, at_tm(1))
-    corner.start()
-    partial = [
-        remote(p_send.at[pl.ds(i * size, size)], p_recv.at[pl.ds(i * size, size)], ps_sem.at[i], pr_sem.at[i], at_tm(1))
-        for i in range(2)
+    halves = [pl.ds(i * size, size) for i in range(2)]
+    sent = [
+        (z_most, z_scale, at_tile(1)), (z_send, z_recv, at_tile(1)),
+        (p_most, p_scale, at_tm(1)), (p_send.at[halves[0]], p_recv.at[halves[0]], at_tm(1)),
+        (p_send.at[halves[1]], p_recv.at[halves[1]], at_tm(1)),
+        (c_most, c_scale, aslant(1)), (c_send, c_recv, aslant(1)),
     ]
-    for copy in partial:
+    halo = [remote(src, dst, halo_send.at[i], halo_recv.at[i], to) for i, (src, dst, to) in enumerate(sent)]
+    pl.semaphore_wait(barrier, n_tile - 1 + len(reach) + 2)
+    for copy in halo:
         copy.start()
-
-    edge = [remote(z_send.at[k], z_recv.at[k], zs_sem.at[k], zr_sem.at[k], at_tile(1)) for k in range(4)]
 
     ready(0)
     ready(4)
     ready(5)
-    z_send[3] = below(((0, 4), (1, 5), (2, 6)))
-    z_first = below(((2, 0),))
-    z_own = below(((0, 0), (1, 0)))
     taps(((2, 0),), y.at[0])
-    taps(((0, 0), (1, 0)), p_own)
     taps(((0, 4), (1, 5), (2, 6)), y.at[3])
-    edge[3].start()
-
-    corner.wait_recv()
-    z_send[0] = z_first + jnp.where(opens[0], z_own, c_recv[...])
-    edge[0].start()
 
     ready(2)
     loads[3].wait()
     pair_columns(lambda r: jnp.where(opens[1], xb[4, r], xb[3, r]), 3)
     pair_columns(lambda r: jnp.where(opens[1], xb[4, r], xb[2, r]), 8)
     ready(1)
-    z_send[2] = below(((0, 8), (1, 3), (2, 4)))
-    z_send[1] = below(((0, 0), (1, 1), (2, 2)))
-    edge[2].start()
-    edge[1].start()
     taps(((0, 8), (1, 3), (2, 4)), y.at[2])
     taps(((0, 0), (1, 1), (2, 2)), y.at[1])
 
     def finish(k):
-        edge[k].wait_recv()
-        y[k, 0:cols] = y[k, 0:cols] + jnp.where(tile == 0, 0.0, z_recv[k])
+        above = decode(z_recv, row_of(k), z_scale, k)
         if k == 0:
-            for copy in partial:
+            for copy in halo[2:]:
                 copy.wait_recv()
-            y[k] = y[k] + jnp.where(opens[0], p_own[...], p_recv[...])
+            above = above + jnp.where(opens[0], 0.0, decode(c_recv, row_of(0), c_scale, 0))
+            for r in range(half):
+                there = row_of(r)
+                y[0, there] = y[0, there] + jnp.where(opens[0], p_own[there], decode(p_recv, there, p_scale, r))
+        y[k, 0:cols] = y[k, 0:cols] + jnp.where(tile == 0, 0.0, above)
         mean = jnp.sum(y[k], axis=0, keepdims=True) * (1.0 / m_rows)
         off = y[k] - mean
         return mean, jnp.sum(off * off, axis=0, keepdims=True)
@@ -182,7 +216,11 @@
         return mean, functools.reduce(jnp.add, squares) + count * apart
 
     part = [None] * 4
-    for k in (3, 2, 1, 0):
+    for copy in halo[:2]:
+        copy.wait_recv()
+    part[3] = finish(3)
+    taps(((0, 0), (1, 0)), p_own)
+    for k in (2, 1, 0):
         part[k] = finish(k)
     count = m_rows
     blocks = [pool([part[2 * m][0], part[2 * m + 1][0]], [part[2 * m][1], part[2 * m + 1][1]], count) for m in range(CH_DEV)]
@@ -195,7 +233,7 @@
 
     mine[...] = packed(blocks)
     to_tiles = [
-        remote(mine, from_tile.at[k - 1], as_sem.at[k - 1], ar_sem.at[k - 1], at_tile(k)) for k in range(1, n_tile)
+        remote(mine, from_tile.at[k - 1], as_sem.at[k - 1], ar_sem.at[k - 1], at_tile(k)) for k in around
     ]
     for copy in to_tiles:
         copy.start()
@@ -241,8 +279,7 @@
         rows_out += [mean, lax.rsqrt(variance + EPS)]
     stat_out[...] = jnp.concatenate(rows_out + [fill], axis=0)
 
-    corner.wait_send()
-    for copy in partial + edge + to_tiles + to_tm:
+    for copy in halo + to_tiles + to_tm:
         copy.wait_send()
 
 
@@ -276,23 +313,26 @@
         out_specs=[vmem, vmem],
         scratch_shapes=[
             pltpu.SMEM(clip_spans.shape, jnp.int32),
+            pltpu.VMEM((frames, width, chans), bf16),
+            pltpu.VMEM((frames, cols, 2 * chans), bf16),
             pltpu.VMEM((frames, rows, width, chans), bf16),
             pltpu.VMEM((frames + 1, half, cols, 2 * chans), bf16),
             pltpu.VMEM((frames + 1, half + 1, cols, 2 * chans), bf16),
             pltpu.VMEM((9, 2 * chans, 2 * chans), bf16),
             pltpu.VMEM((m_rows, chans), f32),
             pltpu.VMEM((m_rows, chans), f32),
-            pltpu.VMEM((cols, chans), f32),
-            pltpu.VMEM((m_rows, chans), f32),
-            pltpu.VMEM((cols, chans), f32),
-            pltpu.VMEM((outs, cols, chans), f32),
-            pltpu.VMEM((outs, cols, chans), f32),
+            *[
+                pltpu.VMEM((n, chans), kind)
+                for _ in range(2)
+                for n, kind in (
+                    (m_rows, jnp.int16), (half, f32), (cols, jnp.int16), (8, f32), (outs * cols, jnp.int16), (8, f32)
+                )
+            ],
             pltpu.VMEM((8, chans), f32),
             pltpu.VMEM((n_tile - 1, 8, chans), f32),
             pltpu.VMEM((8, chans), f32),
             pltpu.VMEM((n_reach, 8, chans), f32),
-            dma, dma((frames,)), dma((3,)),
-            dma((2,)), dma((2,)), dma, dma, dma((4,)), dma((4,)),
+            dma, dma, dma((frames,)), dma((3, 3)), dma((7,)), dma((7,)),
             dma((n_tile - 1,)), dma((n_tile - 1,)), dma((n_reach,)), dma((n_reach,)),
         ],
         compiler_params=pltpu.CompilerParams(

time: 33.5 us -> 29.3 us (0.87)
  Pallas kernels: 33.4 us -> 29.2 us
    pallas_call x1, Pallas kernels: 32 us -> 27.8 us  [body(): pl.pallas_call(functools.partial(kernel, n_tm, n_tile, rows, cols, chans)...]
where the time goes in v3:
time: 29.3 us; the launch traced here: 29.2 us
  Pallas kernels  29.2 us (100%)
    pallas_call x1, Pallas kernels, body(): pl.pallas_call(functools.partial(kernel, n_tm, n_tile, rows, cols, chans)...  27.8 us
    pallas_call x1, Pallas kernels, body(): pl.pallas_call(finishing, out_shape=jax.ShapeDtypeStruct((outs, m_rows, c...  1.33 us

profile of v3, /device:TPU:1, one launch (start us, length us, event | category | flops | bytes accessed | tf_op | source)
XLA Modules:
  0.0 29.2 jit_solution(11814375413577773983)
XLA Ops:
  0.0 0.0 copy-start.1
  0.0 0.0 copy-start
  0.0 27.8 %shard_map.55 = (f32[4,1024,128]{2,1,0:T(8,128)S(1)}, f32[8,128]{1,0:T(8,128)S(1)}) custom-call(s32[16]{0:T(128)} %spans_hbm.1, bf16[8,16,256,128]{3,2,1,0:T(8,128)(2,1)} %x_hbm.1, bf16[9,3,128,128]{3,2,1,0:T(8,128)(2,1)} %bitcast.6), custom_call_target="tpu_custom_call" | custom-call | tf_op jit(solution)/shard_map/pallas_call | solution.py:309
  27.8 0.0 copy-done.1
  27.9 0.0 copy-done
  27.9 1.3 %shard_map.56 = bf16[4,1024,128]{2,1,0:T(8,128)(2,1)} custom-call(f32[4,1024,128]{2,1,0:T(8,128)S(1)} %get-tuple-element.7.y, f32[8,128]{1,0:T(8,128)S(1)} %get-tuple-element.8.stats, f32[1,128]{1,0:T(1,128)S(1)} %bitcast.4, f32[1,128]{1,0:T(1,128)S(1)} %bitcast.5), custom_call_target="tpu_custom_call" | custom-call | tf_op jit(solution)/shard_map/pallas_call | solution.py:346
Async XLA Ops:
  0.0 27.8 %copy-start.1 = (f32[128]{0:T(128)S(1)}, f32[128]{0:T(128)}, u32[]{:S(2)}) copy-start(f32[128]{0:T(128)} %param.9) | copy-start | bytes 1540
  0.0 27.9 %copy-start = (f32[128]{0:T(128)S(1)}, f32[128]{0:T(128)}, u32[]{:S(2)}) copy-start(f32[128]{0:T(128)} %param.8) | copy-start | bytes 1540

commit v4 on v3

--- a/solution.py
+++ b/solution.py
@@ -36,10 +36,39 @@
         return {"tm": lax.rem(tm + k + n_tm, n_tm)}
 
     def at_tile(k):
-        return {"tile": lax.rem(tile + k, n_tile)}
+        return {"tile": lax.rem(tile + k + n_tile, n_tile)}
 
     def aslant(k):
-        return {"tm": lax.rem(tm + k + n_tm, n_tm), "tile": lax.rem(tile + k + n_tile, n_tile)}
+        return at_tm(k) | at_tile(k)
+
+    def has_tm(k):
+        return jnp.logical_and(tm + k >= 0, tm + k < n_tm)
+
+    def has_tile(k):
+        return jnp.logical_and(tile + k >= 0, tile + k < n_tile)
+
+    def has_both(k):
+        return jnp.logical_and(has_tm(k), has_tile(k))
+
+    def greet(there, to):
+        @pl.when(there)
+        def _():
+            pl.semaphore_signal(barrier, inc=1, device_id=to, device_id_type=MESH)
+
+    def start(copy, there):
+        @pl.when(there)
+        def _():
+            copy.start()
+
+    def wait_recv(copy, there):
+        @pl.when(there)
+        def _():
+            copy.wait_recv()
+
+    def wait_send(copy, there):
+        @pl.when(there)
+        def _():
+            copy.wait_send()
 
     def remote(src, dst, send, recv, where):
         return pltpu.make_async_remote_copy(
@@ -66,13 +95,19 @@
     for f in order:
         loads[f].start()
 
+    for ref in (p_scale, c_scale, z_scale, from_tm):
+        ref[...] = jnp.zeros_like(ref)
+
     barrier = pltpu.get_barrier_semaphore()
-    for k in range(1, n_tile):
+    met = jnp.int32(n_tile - 1)
+    for k in around:
         pl.semaphore_signal(barrier, inc=1, device_id=at_tile(k), device_id_type=MESH)
     for k in reach:
-        pl.semaphore_signal(barrier, inc=1, device_id=at_tm(k), device_id_type=MESH)
+        greet(has_tm(k), at_tm(k))
+        met = met + has_tm(k).astype(jnp.int32)
     for k in (-1, 1):
-        pl.semaphore_signal(barrier, inc=1, device_id=aslant(k), device_id_type=MESH)
+        greet(has_both(k), aslant(k))
+        met = met + has_both(k).astype(jnp.int32)
 
     spans_load.wait()
     ends, total = [], jnp.int32(0)
@@ -171,16 +206,19 @@
         encode(p_raw[row_of(r)], p_send, row_of(r), p_most, r)
     size = m_rows // 2
     halves = [pl.ds(i * size, size) for i in range(2)]
+    above_on, last_on, corner_on = ((has_tile(1), has_tile(-1)), (has_tm(1), has_tm(-1)), (has_both(1), has_both(-1)))
     sent = [
-        (z_most, z_scale, at_tile(1)), (z_send, z_recv, at_tile(1)),
-        (p_most, p_scale, at_tm(1)), (p_send.at[halves[0]], p_recv.at[halves[0]], at_tm(1)),
-        (p_send.at[halves[1]], p_recv.at[halves[1]], at_tm(1)),
-        (c_most, c_scale, aslant(1)), (c_send, c_recv, aslant(1)),
+        (z_most, z_scale, at_tile(1), above_on), (z_send, z_recv, at_tile(1), above_on),
+        (p_most, p_scale, at_tm(1), last_on), (p_send.at[halves[0]], p_recv.at[halves[0]], at_tm(1), last_on),
+        (p_send.at[halves[1]], p_recv.at[halves[1]], at_tm(1), last_on),
+        (c_most, c_scale, aslant(1), corner_on), (c_send, c_recv, aslant(1), corner_on),
     ]
-    halo = [remote(src, dst, halo_send.at[i], halo_recv.at[i], to) for i, (src, dst, to) in enumerate(sent)]
-    pl.semaphore_wait(barrier, n_tile - 1 + len(reach) + 2)
-    for copy in halo:
-        copy.start()
+    halo = [
+        (remote(src, dst, halo_send.at[i], halo_recv.at[i], to), *on) for i, (src, dst, to, on) in enumerate(sent)
+    ]
+    pl.semaphore_wait(barrier, met)
+    for copy, out_on, _ in halo:
+        start(copy, out_on)
 
     ready(0)
     ready(4)
@@ -199,8 +237,8 @@
     def finish(k):
         above = decode(z_recv, row_of(k), z_scale, k)
         if k == 0:
-            for copy in halo[2:]:
-                copy.wait_recv()
+            for copy, _, in_on in halo[2:]:
+                wait_recv(copy, in_on)
             above = above + jnp.where(opens[0], 0.0, decode(c_recv, row_of(0), c_scale, 0))
             for r in range(half):
                 there = row_of(r)
@@ -216,8 +254,8 @@
         return mean, functools.reduce(jnp.add, squares) + count * apart
 
     part = [None] * 4
-    for copy in halo[:2]:
-        copy.wait_recv()
+    for copy, _, in_on in halo[:2]:
+        wait_recv(copy, in_on)
     part[3] = finish(3)
     taps(((0, 0), (1, 0)), p_own)
     for k in (2, 1, 0):
@@ -246,10 +284,10 @@
     pooled[...] = jnp.concatenate([mean, square, fill], axis=0)
 
     to_tm = [remote(pooled, from_tm.at[i], bs_sem.at[i], br_sem.at[i], at_tm(k)) for i, k in enumerate(reach)]
-    for copy in to_tm:
-        copy.start()
-    for copy in to_tm:
-        copy.wait_recv()
+    for copy, k in zip(to_tm, reach):
+        start(copy, has_tm(k))
+    for copy, k in zip(to_tm, reach):
+        wait_recv(copy, has_tm(-k))
     held = [(tm, pooled[...])] + [(tm - k, from_tm[i]) for i, k in enumerate(reach)]
 
     lane = lax.broadcasted_iota(jnp.int32, (1, chans), 1)
@@ -279,8 +317,12 @@
         rows_out += [mean, lax.rsqrt(variance + EPS)]
     stat_out[...] = jnp.concatenate(rows_out + [fill], axis=0)
 
-    for copy in halo + to_tiles + to_tm:
+    for copy, out_on, _ in halo:
+        wait_send(copy, out_on)
+    for copy in to_tiles:
         copy.wait_send()
+    for copy, k in zip(to_tm, reach):
+        wait_send(copy, has_tm(k))
 
 
 def finishing(y, stats, gain, bias, out_hbm, out, sem):

time: 29.3 us -> 27.1 us (0.925)
  Pallas kernels: 29.2 us -> 27 us
    pallas_call x1, Pallas kernels: 27.8 us -> 25.6 us  [body(): pl.pallas_call(functools.partial(kernel, n_tm, n_tile, rows, cols, chans)...]
where the time goes in v4:
time: 27.1 us; the launch traced here: 27 us
  Pallas kernels  27 us (100%)
    pallas_call x1, Pallas kernels, body(): pl.pallas_call(functools.partial(kernel, n_tm, n_tile, rows, cols, chans)...  25.6 us
    pallas_call x1, Pallas kernels, body(): pl.pallas_call(finishing, out_shape=jax.ShapeDtypeStruct((outs, m_rows, c...  1.33 us

profile of v4, /device:TPU:1, one launch (start us, length us, event | category | flops | bytes accessed | tf_op | source)
XLA Modules:
  0.0 27.0 jit_solution(1079418256918665730)
XLA Ops:
  0.0 0.0 copy-start.1
  0.0 0.0 copy-start
  0.0 25.6 %shard_map.55 = (f32[4,1024,128]{2,1,0:T(8,128)S(1)}, f32[8,128]{1,0:T(8,128)S(1)}) custom-call(s32[16]{0:T(128)} %spans_hbm.1, bf16[8,16,256,128]{3,2,1,0:T(8,128)(2,1)} %x_hbm.1, bf16[9,3,128,128]{3,2,1,0:T(8,128)(2,1)} %bitcast.6), custom_call_target="tpu_custom_call" | custom-call | tf_op jit(solution)/shard_map/pallas_call | solution.py:351
  25.7 0.0 copy-done.1
  25.7 0.0 copy-done
  25.7 1.3 %shard_map.56 = bf16[4,1024,128]{2,1,0:T(8,128)(2,1)} custom-call(f32[4,1024,128]{2,1,0:T(8,128)S(1)} %get-tuple-element.7.y, f32[8,128]{1,0:T(8,128)S(1)} %get-tuple-element.8.stats, f32[1,128]{1,0:T(1,128)S(1)} %bitcast.4, f32[1,128]{1,0:T(1,128)S(1)} %bitcast.5), custom_call_target="tpu_custom_call" | custom-call | tf_op jit(solution)/shard_map/pallas_call | solution.py:388
Async XLA Ops:
  0.0 25.7 %copy-start.1 = (f32[128]{0:T(128)S(1)}, f32[128]{0:T(128)}, u32[]{:S(2)}) copy-start(f32[128]{0:T(128)} %param.9) | copy-start | bytes 1540
  0.0 25.7 %copy-start = (f32[128]{0:T(128)S(1)}, f32[128]{0:T(128)}, u32[]{:S(2)}) copy-start(f32[128]{0:T(128)} %param.8) | copy-start | bytes 1540

commit v5 on v4

--- a/solution.py
+++ b/solution.py
@@ -200,8 +200,9 @@
     encode(aside, c_send, row_of(0), c_most, 0)
 
     ready(6)
+    taps(((0, 6),), p_raw)
     ready(7)
-    taps(((0, 6), (1, 7)), p_raw)
+    taps(((1, 7),), p_raw, add=True)
     for r in range(half):
         encode(p_raw[row_of(r)], p_send, row_of(r), p_most, r)
     size = m_rows // 2
@@ -224,6 +225,7 @@
     ready(4)
     ready(5)
     taps(((2, 0),), y.at[0])
+    taps(((0, 0),), p_own)
     taps(((0, 4), (1, 5), (2, 6)), y.at[3])
 
     ready(2)
@@ -232,7 +234,8 @@
     pair_columns(lambda r: jnp.where(opens[1], xb[4, r], xb[2, r]), 8)
     ready(1)
     taps(((0, 8), (1, 3), (2, 4)), y.at[2])
-    taps(((0, 0), (1, 1), (2, 2)), y.at[1])
+    y[1] = p_own[...]
+    taps(((1, 1), (2, 2)), y.at[1], add=True)
 
     def finish(k):
         above = decode(z_recv, row_of(k), z_scale, k)
@@ -257,7 +260,7 @@
     for copy, _, in_on in halo[:2]:
         wait_recv(copy, in_on)
     part[3] = finish(3)
-    taps(((0, 0), (1, 0)), p_own)
+    taps(((1, 0),), p_own, add=True)
     for k in (2, 1, 0):
         part[k] = finish(k)
     count = m_rows

time: 27.1 us -> 26.5 us (0.978)
  Pallas kernels: 27 us -> 26.4 us
    pallas_call x1, Pallas kernels: 25.6 us -> 25.1 us  [body(): pl.pallas_call(functools.partial(kernel, n_tm, n_tile, rows, cols, chans)...]
where the time goes in v5:
time: 26.5 us; the launch traced here: 26.4 us
  Pallas kernels  26.4 us (100%)
    pallas_call x1, Pallas kernels, body(): pl.pallas_call(functools.partial(kernel, n_tm, n_tile, rows, cols, chans)...  25.1 us
    pallas_call x1, Pallas kernels, body(): pl.pallas_call(finishing, out_shape=jax.ShapeDtypeStruct((outs, m_rows, c...  1.33 us

profile of v5, /device:TPU:1, one launch (start us, length us, event | category | flops | bytes accessed | tf_op | source)
XLA Modules:
  0.0 26.4 jit_solution(2546109339619996412)
XLA Ops:
  0.0 0.0 copy-start.1
  0.0 0.0 copy-start
  0.0 25.1 %shard_map.55 = (f32[4,1024,128]{2,1,0:T(8,128)S(1)}, f32[8,128]{1,0:T(8,128)S(1)}) custom-call(s32[16]{0:T(128)} %spans_hbm.1, bf16[8,16,256,128]{3,2,1,0:T(8,128)(2,1)} %x_hbm.1, bf16[9,3,128,128]{3,2,1,0:T(8,128)(2,1)} %bitcast.6), custom_call_target="tpu_custom_call" | custom-call | tf_op jit(solution)/shard_map/pallas_call | solution.py:354
  25.1 0.0 copy-done.1
  25.1 0.0 copy-done
  25.1 1.3 %shard_map.56 = bf16[4,1024,128]{2,1,0:T(8,128)(2,1)} custom-call(f32[4,1024,128]{2,1,0:T(8,128)S(1)} %get-tuple-element.7.y, f32[8,128]{1,0:T(8,128)S(1)} %get-tuple-element.8.stats, f32[1,128]{1,0:T(1,128)S(1)} %bitcast.4, f32[1,128]{1,0:T(1,128)S(1)} %bitcast.5), custom_call_target="tpu_custom_call" | custom-call | tf_op jit(solution)/shard_map/pallas_call | solution.py:391
Async XLA Ops:
  0.0 25.1 %copy-start.1 = (f32[128]{0:T(128)S(1)}, f32[128]{0:T(128)}, u32[]{:S(2)}) copy-start(f32[128]{0:T(128)} %param.9) | copy-start | bytes 1540
  0.0 25.1 %copy-start = (f32[128]{0:T(128)S(1)}, f32[128]{0:T(128)}, u32[]{:S(2)}) copy-start(f32[128]{0:T(128)} %param.8) | copy-start | bytes 1540

commit v6 on v5

--- a/solution.py
+++ b/solution.py
@@ -278,6 +278,8 @@
     ]
     for copy in to_tiles:
         copy.start()
+    for copy, out_on, _ in halo:
+        wait_send(copy, out_on)
     for copy in to_tiles:
         copy.wait_recv()
     all_means = [mine[0:CH_DEV]] + [from_tile[k, 0:CH_DEV] for k in range(n_tile - 1)]
@@ -289,6 +291,8 @@
     to_tm = [remote(pooled, from_tm.at[i], bs_sem.at[i], br_sem.at[i], at_tm(k)) for i, k in enumerate(reach)]
     for copy, k in zip(to_tm, reach):
         start(copy, has_tm(k))
+    for copy in to_tiles:
+        copy.wait_send()
     for copy, k in zip(to_tm, reach):
         wait_recv(copy, has_tm(-k))
     held = [(tm, pooled[...])] + [(tm - k, from_tm[i]) for i, k in enumerate(reach)]
@@ -320,10 +324,6 @@
         rows_out += [mean, lax.rsqrt(variance + EPS)]
     stat_out[...] = jnp.concatenate(rows_out + [fill], axis=0)
 
-    for copy, out_on, _ in halo:
-        wait_send(copy, out_on)
-    for copy in to_tiles:
-        copy.wait_send()
     for copy, k in zip(to_tm, reach):
         wait_send(copy, has_tm(k))
 

time: 26.5 us -> 26.5 us (level)
  no operation moved by 1% of the time
where the time goes in v6:
time: 26.5 us; the launch traced here: 26.4 us
  Pallas kernels  26.4 us (100%)
    pallas_call x1, Pallas kernels, body(): pl.pallas_call(functools.partial(kernel, n_tm, n_tile, rows, cols, chans)...  25 us
    pallas_call x1, Pallas kernels, body(): pl.pallas_call(finishing, out_shape=jax.ShapeDtypeStruct((outs, m_rows, c...  1.33 us

profile of v6, /device:TPU:1, one launch (start us, length us, event | category | flops | bytes accessed | tf_op | source)
XLA Modules:
  0.0 26.4 jit_solution(17839278717698928030)
XLA Ops:
  0.0 0.0 copy-start.1
  0.0 0.0 copy-start
  0.0 25.0 %shard_map.55 = (f32[4,1024,128]{2,1,0:T(8,128)S(1)}, f32[8,128]{1,0:T(8,128)S(1)}) custom-call(s32[16]{0:T(128)} %spans_hbm.1, bf16[8,16,256,128]{3,2,1,0:T(8,128)(2,1)} %x_hbm.1, bf16[9,3,128,128]{3,2,1,0:T(8,128)(2,1)} %bitcast.6), custom_call_target="tpu_custom_call" | custom-call | tf_op jit(solution)/shard_map/pallas_call | solution.py:354
  25.1 0.0 copy-done.1
  25.1 0.0 copy-done
  25.1 1.3 %shard_map.56 = bf16[4,1024,128]{2,1,0:T(8,128)(2,1)} custom-call(f32[4,1024,128]{2,1,0:T(8,128)S(1)} %get-tuple-element.7.y, f32[8,128]{1,0:T(8,128)S(1)} %get-tuple-element.8.stats, f32[1,128]{1,0:T(1,128)S(1)} %bitcast.4, f32[1,128]{1,0:T(1,128)S(1)} %bitcast.5), custom_call_target="tpu_custom_call" | custom-call | tf_op jit(solution)/shard_map/pallas_call | solution.py:391
Async XLA Ops:
  0.0 25.1 %copy-start.1 = (f32[128]{0:T(128)S(1)}, f32[128]{0:T(128)}, u32[]{:S(2)}) copy-start(f32[128]{0:T(128)} %param.9) | copy-start | bytes 1540
  0.0 25.1 %copy-start = (f32[128]{0:T(128)S(1)}, f32[128]{0:T(128)}, u32[]{:S(2)}) copy-start(f32[128]{0:T(128)} %param.8) | copy-start | bytes 1540

commit v7 on v6

--- a/solution.py
+++ b/solution.py
@@ -14,6 +14,7 @@
 EPS = 1e-6
 CODES = 32767.0
 TINY = 1e-30
+PARTS = 2
 MESH = pl.DeviceIdType.MESH
 f32, bf16 = jnp.float32, jnp.bfloat16
 
@@ -218,7 +219,7 @@
         (remote(src, dst, halo_send.at[i], halo_recv.at[i], to), *on) for i, (src, dst, to, on) in enumerate(sent)
     ]
     pl.semaphore_wait(barrier, met)
-    for copy, out_on, _ in halo:
+    for copy, out_on, _ in halo[2:] + halo[:2]:
         start(copy, out_on)
 
     ready(0)
@@ -330,12 +331,14 @@
 
 def finishing(y, stats, gain, bias, out_hbm, out, sem):
     copies = []
-    for k in range(y.shape[0]):
+    part = y.shape[1] // PARTS
+    for i in range(y.shape[0] * PARTS):
+        k, rows = i // PARTS, pl.ds(i % PARTS * part, part)
         m = k // (F // 2)
-        normed = (y[k] - stats[2 * m : 2 * m + 1]) * stats[2 * m + 1 : 2 * m + 2] * gain[...] + bias[...]
+        normed = (y[k, rows] - stats[2 * m : 2 * m + 1]) * stats[2 * m + 1 : 2 * m + 2] * gain[...] + bias[...]
         halved = 0.5 * normed
-        out[k] = (halved * jnp.tanh(halved) + halved).astype(bf16)
-        copies.append(pltpu.make_async_copy(out.at[k], out_hbm.at[k], sem.at[k]))
+        out[k, rows] = (halved * jnp.tanh(halved) + halved).astype(bf16)
+        copies.append(pltpu.make_async_copy(out.at[k, rows], out_hbm.at[k, rows], sem.at[i]))
         copies[-1].start()
     for copy in copies:
         copy.wait()
@@ -393,7 +396,7 @@
         out_shape=jax.ShapeDtypeStruct((outs, m_rows, chans), bf16),
         in_specs=[vmem] * 4,
         out_specs=any_space,
-        scratch_shapes=[pltpu.VMEM((outs, m_rows, chans), bf16), dma((outs,))],
+        scratch_shapes=[pltpu.VMEM((outs, m_rows, chans), bf16), dma((outs * PARTS,))],
         compiler_params=pltpu.CompilerParams(vmem_limit_bytes=16 * 2**20),
     )(
         pltpu.with_memory_space_constraint(y, pltpu.VMEM),

time: 26.5 us -> 26.7 us (level)
  no operation moved by 1% of the time
where the time goes in v7:
time: 26.7 us; the launch traced here: 26.6 us
  Pallas kernels  26.6 us (100%)
    pallas_call x1, Pallas kernels, body(): pl.pallas_call(functools.partial(kernel, n_tm, n_tile, rows, cols, chans)...  25.2 us
    pallas_call x1, Pallas kernels, body(): pl.pallas_call(finishing, out_shape=jax.ShapeDtypeStruct((outs, m_rows, c...  1.31 us

profile of v7, /device:TPU:1, one launch (start us, length us, event | category | flops | bytes accessed | tf_op | source)
XLA Modules:
  0.0 26.6 jit_solution(11671512537182211027)
XLA Ops:
  0.0 0.0 copy-start.1
  0.0 0.0 copy-start
  0.0 25.2 %shard_map.55 = (f32[4,1024,128]{2,1,0:T(8,128)S(1)}, f32[8,128]{1,0:T(8,128)S(1)}) custom-call(s32[16]{0:T(128)} %spans_hbm.1, bf16[8,16,256,128]{3,2,1,0:T(8,128)(2,1)} %x_hbm.1, bf16[9,3,128,128]{3,2,1,0:T(8,128)(2,1)} %bitcast.6), custom_call_target="tpu_custom_call" | custom-call | tf_op jit(solution)/shard_map/pallas_call | solution.py:357
  25.3 0.0 copy-done.1
  25.3 0.0 copy-done
  25.3 1.3 %shard_map.56 = bf16[4,1024,128]{2,1,0:T(8,128)(2,1)} custom-call(f32[4,1024,128]{2,1,0:T(8,128)S(1)} %get-tuple-element.7.y, f32[8,128]{1,0:T(8,128)S(1)} %get-tuple-element.8.stats, f32[1,128]{1,0:T(1,128)S(1)} %bitcast.4, f32[1,128]{1,0:T(1,128)S(1)} %bitcast.5), custom_call_target="tpu_custom_call" | custom-call | tf_op jit(solution)/shard_map/pallas_call | solution.py:394
Async XLA Ops:
  0.0 25.3 %copy-start.1 = (f32[128]{0:T(128)S(1)}, f32[128]{0:T(128)}, u32[]{:S(2)}) copy-start(f32[128]{0:T(128)} %param.9) | copy-start | bytes 1540
  0.0 25.3 %copy-start = (f32[128]{0:T(128)S(1)}, f32[128]{0:T(128)}, u32[]{:S(2)}) copy-start(f32[128]{0:T(128)} %param.8) | copy-start | bytes 1540
